TPU v7x, 256 devices: a whole 4x4x8 slice. The times are simulated.
256 devices in a mesh: dp: 8 (over y, core), label: 32 (over x, z).
Axes of the slice: x: 4, y: 4, z: 8, core: 2. Of those that a mesh axis runs over, the one named last changes fastest.
Arguments:
- encoded: bfloat16 [32768, 1024], P(('dp', 'label')), may hold values from -6 to 6
- positive_clusters: int32 [32768, 4], P(('dp', 'label')), may hold values from 0 to 16383
- cluster_weight: bfloat16 [16384, 1024], P('label'), may hold values from -0.1875 to 0.1875
- shortlist: int32 [32768, 4], P(('dp', 'label')), may hold values from 0 to 511, all different within a row; in each aligned block of 128 rows (0 to 127, 128 to 255, ...) at most 2 rows name the same one
- positive_offsets: int32 [32768, 4], P(('dp', 'label')), may hold values from 0 to 127
- block_weight: bfloat16 [512, 128, 1024], P('label'), may hold values from -0.1875 to 0.1875
Outputs:
- grad_hidden: bfloat16 [32768, 1024], P(('dp', 'label'))
- grad_cluster: float32 [16384, 1024], P('label', 'dp')
- grad_block: float32 [512, 128, 1024], P('label', None, 'dp')
Inputs may be any that keep to these rules, and one draw needn't show every extreme that they name: `shortlist`: each row names 4 different blocks. Among the rows of one device no block is named more than 2 times, and in every draw some block is named exactly 2 times by the rows of some device.
All inputs are finite; a program needn't handle non-finite values.
Results may differ from a plain program's by a relative error of at most 0.018.
Values may be sent and summed in bfloat16 or wider, within the bound.
A program may use at most 128 MiB of HBM per device.

v0:
```python
import math
import jax
import jax.numpy as jnp
from jax import lax
from jax.sharding import PartitionSpec as P


def per_device(
    encoded, positive_clusters, cluster_weight, shortlist, positive_offsets, block_weight
):
    doc_rows, width = encoded.shape
    label_count = lax.axis_size("label")
    label_index = lax.axis_index("label")
    clusters_dev = cluster_weight.shape[0]
    rows_all = doc_rows * label_count
    scale = 1.0 / math.sqrt(rows_all * lax.axis_size("dp"))
    cluster_ids = label_index * clusters_dev + jnp.arange(clusters_dev, dtype=jnp.int32)
    rows = lax.all_gather(encoded, "label", axis=0, tiled=True)
    positives = lax.all_gather(positive_clusters, "label", axis=0, tiled=True)
    scores = lax.dot_general(
        rows, cluster_weight, (((1,), (1,)), ((), ())), preferred_element_type=jnp.float32
    )
    hits = jnp.any(positives[:, :, None] == cluster_ids[None, None, :], axis=1)
    delta = (jax.nn.sigmoid(scores) - hits.astype(jnp.float32)).astype(jnp.bfloat16)
    grad_sum = lax.dot_general(
        delta, rows, (((0,), (0,)), ((), ())), preferred_element_type=jnp.float32
    )
    deltas = delta
    grad_cluster, deltas = (grad_sum, deltas)
    products = jnp.dot(deltas, cluster_weight, preferred_element_type=jnp.float32)
    hidden_one = lax.psum_scatter(
        products.astype(jnp.bfloat16), "label", scatter_dimension=0, tiled=True
    ).astype(jnp.float32)
    listed = shortlist.shape[1]
    pairs = doc_rows * listed
    blocks_dev, block_len, _ = block_weight.shape
    blocks_total = blocks_dev * label_count
    capacity = max(2, 2 * pairs // blocks_total)
    slots_total = blocks_total * capacity
    flat_block = shortlist.reshape(-1)
    onehot = (flat_block[:, None] == jnp.arange(blocks_total, dtype=jnp.int32)[None, :]).astype(
        jnp.bfloat16
    )
    lower = (jnp.arange(pairs)[:, None] > jnp.arange(pairs)[None, :]).astype(jnp.bfloat16)
    earlier = jnp.dot(lower, onehot, preferred_element_type=jnp.float32)
    rank = jnp.sum(earlier * onehot.astype(jnp.float32), axis=1).astype(jnp.int32)
    slot = flat_block * capacity + rank
    source = (
        jnp.full((slots_total,), -1, jnp.int32).at[slot].set(jnp.arange(pairs, dtype=jnp.int32))
    )
    filled = source >= 0
    picked = jnp.maximum(source, 0)
    send_rows = jnp.where(filled[:, None], encoded[picked // listed], jnp.zeros((), jnp.bfloat16))
    send_offsets = jnp.where(filled, positive_offsets.reshape(-1)[picked], -1)
    send_rows = send_rows.reshape(label_count, blocks_dev * capacity, width)
    send_offsets = send_offsets.reshape(label_count, blocks_dev * capacity)
    got_rows, got_offsets = (
        lax.all_to_all(send_rows, "label", split_axis=0, concat_axis=0, tiled=True),
        lax.all_to_all(send_offsets, "label", split_axis=0, concat_axis=0, tiled=True),
    )
    arrived = got_rows.reshape(label_count, blocks_dev, capacity, width)
    offsets = got_offsets.reshape(label_count, blocks_dev, capacity)
    scores = jnp.einsum("sbcd,bld->sbcl", arrived, block_weight, preferred_element_type=jnp.float32)
    target = (offsets[..., None] == jnp.arange(block_len, dtype=jnp.int32)).astype(jnp.float32)
    delta = jnp.where((offsets >= 0)[..., None], jax.nn.sigmoid(scores) - target, 0.0).astype(
        jnp.bfloat16
    )
    back = jnp.einsum(
        "sbcl,bld->sbcd", delta, block_weight, preferred_element_type=jnp.float32
    ).astype(jnp.bfloat16)
    grad_block = jnp.einsum("sbcl,sbcd->bld", delta, arrived, preferred_element_type=jnp.float32)
    returned = lax.all_to_all(
        back.reshape(label_count, blocks_dev * capacity, width),
        "label",
        split_axis=0,
        concat_axis=0,
        tiled=True,
    )
    per_pair = returned.reshape(slots_total, width)[slot].astype(jnp.float32)
    hidden_two = jnp.sum(per_pair.reshape(doc_rows, listed, width), axis=1)
    grad_hidden = (hidden_one + hidden_two).astype(jnp.bfloat16)
    cluster_share, block_share = (
        lax.psum_scatter(
            (grad_cluster * scale).astype(jnp.bfloat16), "dp", scatter_dimension=1, tiled=True
        ).astype(jnp.float32),
        lax.psum_scatter(
            (grad_block * scale).reshape(blocks_dev * block_len, width).astype(jnp.bfloat16),
            "dp",
            scatter_dimension=1,
            tiled=True,
        ).astype(jnp.float32),
    )
    return (grad_hidden, cluster_share, block_share.reshape(blocks_dev, block_len, -1))


def solution(mesh):
    placed = (
        P(("dp", "label"), None),
        P(("dp", "label"), None),
        P("label", None),
        P(("dp", "label"), None),
        P(("dp", "label"), None),
        P("label", None, None),
    )
    return jax.shard_map(
        per_device,
        mesh=mesh,
        in_specs=placed,
        out_specs=(P(("dp", "label"), None), P("label", "dp"), P("label", None, "dp")),
        check_vma=False,
    )
```

profile of v0, /device:TPU:8, one launch (start us, length us, event | category | flops | bytes accessed | tf_op | source)
XLA Modules:
  0.0 472.1 jit_solution(16597565565228183674)
XLA Ops:
  8.1 0.7 all-gather.2.cloned.1.call-update
  8.8 0.8 copy.38
  9.5 0.7 broadcast_multiply_fusion
  10.2 0.1 copy.37
  10.3 0.1 mul.37
  10.5 0.8 copy.39
  11.2 0.1 reshape.92
  11.4 0.1 eq.42
  11.5 0.5 fusion.8
  12.0 2.4 scatter_custom_fusion
  14.5 6.9 %gather_fusion = s32[1024]{0:T(1024)S(1)} fusion(s32[512]{0:T(512)S(1)} %reshape.92, s32[1024]{0:T(1024)S(1)} %maximum_clamp_fusion), kind=kCustom, calls=%fused_computation | custom fusion | bytes 12288 | tf_op jit(solution)/shard_map/gather | solution.py:54
  21.4 0.7 all_to_all.12
  22.1 11.3 %all-to-all-start = ((s32[32,1,32]{2,1,0:T(1,128)}), s32[32,1,32]{2,1,0:T(1,128)S(1)}, u32[]{:S(2)}, u32[]{:S(2)}) async-start(s32[32,1,32]{2,1,0:T(1,128)} %bitcast.2), calls=%async_computation.1 | async-start | bytes 32768 | tf_op jit(solution)/shard_map/all_to_all | solution.py:59
  33.4 0.1 broadcast_in_dim.50
  33.5 4.1 gather_fusion.1
  37.5 1.6 broadcast_select_fusion
  39.1 4.1 all-to-all-done
  43.2 5.7 %all-to-all-start.1 = ((bf16[32,32,1024]{2,1,0:T(8,128)(2,1)}), bf16[32,32,1024]{2,1,0:T(8,128)(2,1)S(1)}, u32[]{:S(2)}, u32[]{:S(2)}) async-start(bf16[32,32,1024]{2,1,0:T(8,128)(2,1)} %broadcast_select_fusion), calls=%async_computation.2 | async-start | bytes 4194304 | tf_op jit(solution)/shard_map/all_to_all | solution.py:58
  49.0 0.1 copy.41
  49.1 64.0 %all-to-all-done.1 = bf16[32,32,1024]{2,1,0:T(8,128)(2,1)S(1)} async-done(((bf16[32,32,1024]{2,1,0:T(8,128)(2,1)}), bf16[32,32,1024]{2,1,0:T(8,128)(2,1)S(1)}, u32[]{:S(2)}, u32[]{:S(2)}) %all-to-all-start.1) | async-done | bytes 2097184 | tf_op jit(solution)/shard_map/all_to_all | solution.py:58
  113.0 1.2 copy.42
  114.2 1.2 copy-done.2
  115.4 1.7 fusion.30
  117.1 3.2 fusion
  120.4 6.5 %copy.48 = bf16[2048,1024]{0,1:T(8,128)(2,1)} copy(bf16[2048,1024]{1,0:T(8,128)(2,1)} %bitcast.68) | data formatting | bytes 8388608
  126.9 0.0 reduce-scatter.10.cloned.1.call-start
  126.9 0.6 copy-done.3
  127.5 48.2 %all_gather.7 = s32[4096,4]{0,1:T(4,128)S(1)} all-gather(s32[128,4]{0,1:T(4,128)S(1)} %copy-done.3), channel_id=1, replica_groups=mesh['dp'=8,'label'=32] {'label'}, dimensions={0}, use_global_device_ids=true | all-gather | bytes 67584 | tf_op jit(solution)/shard_map/all_gather | solution.py:19
  175.7 5.1 %compare_reduce_fusion = pred[4096,512]{1,0:T(8,128)(4,1)S(1)} fusion(s32[512]{0:T(512)S(1)} %iota_add_fusion, s32[4096,4]{0,1:T(4,128)S(1)} %all_gather.7), kind=kLoop, calls=%fused_computation.4 | loop fusion | flops 14680064 | bytes 2164736 | tf_op jit(solution)/shard_map/reduce_or | solution.py:23
  180.9 9.2 %subtract_convert_fusion = bf16[4096,512]{1,0:T(8,128)(2,1)S(1)} fusion(pred[4096,512]{1,0:T(8,128)(4,1)S(1)} %compare_reduce_fusion, bf16[4096,1024]{1,0:T(8,128)(2,1)} %all-gather.2.cloned.1.call-done, bf16[512,1024]{1,0:T(8,128)(2,1)S(1)} %copy-done), kind=kOutput, calls=%fused_computation.7 | convolution fusion | flops 4307550208 | bytes 15728640 | tf_op jit(solution)/shard_map/dot_general | solution.py:20
  190.1 1.9 copy-done.5
  192.0 4.5 multiply_convert_fusion
  196.5 1.3 copy.46
  197.9 0.3 reduce-scatter.8.cloned.1.call-start
  198.1 9.0 %convolution_convert_fusion = bf16[4096,1024]{1,0:T(8,128)(2,1)} fusion(bf16[4096,512]{1,0:T(8,128)(2,1)} %copy-done.5, bf16[512,1024]{1,0:T(8,128)(2,1)S(1)} %copy-done), kind=kOutput, calls=%fused_computation.8 | convolution fusion | flops 4299161600 | bytes 13631488 | tf_op jit(solution)/shard_map/dot_general | solution.py:30
  207.2 2.9 fusion.5
  210.1 2.5 copy.43
  212.6 5.5 %all-to-all-start.2 = ((bf16[32,32,1024]{2,1,0:T(8,128)(2,1)}), bf16[32,32,1024]{2,1,0:T(8,128)(2,1)S(1)}, u32[]{:S(2)}, u32[]{:S(2)}) async-start(bf16[32,32,1024]{2,1,0:T(8,128)(2,1)} %copy.43), calls=%async_computation.3 | async-start | bytes 4194304 | tf_op jit(solution)/shard_map/all_to_all | solution.py:72
  218.2 39.4 %all-to-all-done.2 = bf16[32,32,1024]{2,1,0:T(8,128)(2,1)S(1)} async-done(((bf16[32,32,1024]{2,1,0:T(8,128)(2,1)}), bf16[32,32,1024]{2,1,0:T(8,128)(2,1)S(1)}, u32[]{:S(2)}, u32[]{:S(2)}) %all-to-all-start.2) | async-done | bytes 2097184 | tf_op jit(solution)/shard_map/all_to_all | solution.py:72
  257.5 2.8 gather_fusion.2
  260.3 1.7 reshape.99
  262.0 2.2 reduce_sum.19
  264.3 1.3 copy.49
  265.6 1.1 convert.2
  266.7 1.0 copy.47
  267.7 0.7 convert_element_type.83
  268.4 194.2 %reduce-scatter.8.cloned.1.call-done = bf16[128,1024]{1,0:T(8,128)(2,1)} async-done(((bf16[4096,1024]{1,0:T(8,128)(2,1)}), bf16[128,1024]{1,0:T(8,128)(2,1)}) %reduce-scatter.8.cloned.1.call-update) | async-done | bytes 262160 | tf_op jit(solution)/shard_map/reduce_scatter | solution.py:31
  462.7 1.9 add_convert_fusion
  (25 shorter events, 0.2 us)
Async XLA Ops:
  8.0 172.9 %copy-start = (bf16[512,1024]{1,0:T(8,128)(2,1)S(1)}, bf16[512,1024]{1,0:T(8,128)(2,1)}, u32[]{:S(2)}) copy-start(bf16[512,1024]{1,0:T(8,128)(2,1)} %param.8) | copy-start | bytes 3145732
  8.0 25.5 %copy-start.1 = (bf16[128,1024]{1,0:T(8,128)(2,1)S(1)}, bf16[128,1024]{1,0:T(8,128)(2,1)}, u32[]{:S(2)}) copy-start(bf16[128,1024]{1,0:T(8,128)(2,1)} %param.6) | copy-start | bytes 786436
  8.0 172.8 %all-gather.2.cloned.1.call-start = ((), (), s32[]{:S(2)}) async-start(), calls=%async_computation.6 | async-start | bytes 8650752 | tf_op jit(solution)/shard_map/all_gather | solution.py:18
  22.1 21.1 %all-to-all-start = ((s32[32,1,32]{2,1,0:T(1,128)}), s32[32,1,32]{2,1,0:T(1,128)S(1)}, u32[]{:S(2)}, u32[]{:S(2)}) async-start(s32[32,1,32]{2,1,0:T(1,128)} %bitcast.2), calls=%async_computation.1 | async-start | bytes 32768 | tf_op jit(solution)/shard_map/all_to_all | solution.py:59
  43.2 69.8 %all-to-all-start.1 = ((bf16[32,32,1024]{2,1,0:T(8,128)(2,1)}), bf16[32,32,1024]{2,1,0:T(8,128)(2,1)S(1)}, u32[]{:S(2)}, u32[]{:S(2)}) async-start(bf16[32,32,1024]{2,1,0:T(8,128)(2,1)} %broadcast_select_fusion), calls=%async_computation.2 | async-start | bytes 4194304 | tf_op jit(solution)/shard_map/all_to_all | solution.py:58
  48.9 215.3 %reduce-scatter.12.cloned.1.call-start = ((), (), s32[]{:S(2)}) async-start(), calls=%async_computation.9 | async-start | bytes 4718592
  113.0 2.3 copy-start.2
  126.8 0.7 copy-start.3
  126.9 139.8 %reduce-scatter.10.cloned.1.call-start = ((), (), s32[]{:S(2)}) async-start(), calls=%async_computation.8 | async-start | bytes 1179648
  180.9 11.1 %copy-start.4 = (bf16[4096,1024]{1,0:T(8,128)(2,1)S(1)}, bf16[4096,1024]{1,0:T(8,128)(2,1)}, u32[]{:S(2)}) copy-start(bf16[4096,1024]{1,0:T(8,128)(2,1)} %all-gather.2.cloned.1.call-done) | copy-start | bytes 25165828
  190.1 1.9 copy-start.5
  197.9 264.8 %reduce-scatter.8.cloned.1.call-start = ((), (), s32[]{:S(2)}) async-start(), calls=%async_computation.7 | async-start | bytes 8650752 | tf_op jit(solution)/shard_map/reduce_scatter | solution.py:31
  212.6 44.9 %all-to-all-start.2 = ((bf16[32,32,1024]{2,1,0:T(8,128)(2,1)}), bf16[32,32,1024]{2,1,0:T(8,128)(2,1)S(1)}, u32[]{:S(2)}, u32[]{:S(2)}) async-start(bf16[32,32,1024]{2,1,0:T(8,128)(2,1)} %copy.43), calls=%async_computation.3 | async-start | bytes 4194304 | tf_op jit(solution)/shard_map/all_to_all | solution.py:72
Sparse Core Ops, SparseCore 0:
  11.4 126.3 all-gather.1
Sparse Core Ops, SparseCore 1:
  126.9 34.5 reduce-scatter.11
  198.0 28.3 reduce-scatter.9
  230.2 232.4 reduce-scatter.7
where the time goes:
time: 473 us; the launch traced here: 472 us
  waiting for transfers between devices  302 us (64%)
  blocking collectives  48.2 us (10%)
  local copies, waits for them, and re-layouts  38.2 us (8%)
  matrix products  31.1 us (7%)
  starting transfers between devices  23 us (5%)
  between operations  15.9 us (3%)
  other arithmetic  13.4 us (3%)
    reduce_scatter x1, waiting for transfers between devices, per_device(): lax.psum_scatter(products.astype(jnp.bfloat16), 'label', scatter_dimensio...  194 us
    all_to_all x1, waiting for transfers between devices, per_device(): lax.all_to_all(send_rows, 'label', split_axis=0, concat_axis=0, tiled=True)  64 us
    all_gather x1, blocking collectives, per_device(): positives = lax.all_gather(positive_clusters, 'label', axis=0, tiled=True)  48.2 us
    all_to_all x1, waiting for transfers between devices, per_device(): lax.all_to_all(back.reshape(label_count, blocks_dev * capacity, width), '...  39.4 us
    unnamed x18, local copies, waits for them, and re-layouts  15.4 us
    all_to_all x1, starting transfers between devices, per_device(): lax.all_to_all(send_offsets, 'label', split_axis=0, concat_axis=0, tiled=...  11.3 us
  transfers between devices with their start and end apart: 7, of which 4 were waited for; matrix products, arithmetic and copies ran while one was open for 16% of the time, Pallas kernels for 0%

commit v1 on v0

--- a/solution.py
+++ b/solution.py
@@ -16,7 +16,10 @@
     scale = 1.0 / math.sqrt(rows_all * lax.axis_size("dp"))
     cluster_ids = label_index * clusters_dev + jnp.arange(clusters_dev, dtype=jnp.int32)
     rows = lax.all_gather(encoded, "label", axis=0, tiled=True)
-    positives = lax.all_gather(positive_clusters, "label", axis=0, tiled=True)
+    positives = jnp.concatenate(
+        lax.all_to_all(jnp.stack([positive_clusters] * lax.axis_size("label")), "label", 0, 0),
+        axis=0,
+    )
     scores = lax.dot_general(
         rows, cluster_weight, (((1,), (1,)), ((), ())), preferred_element_type=jnp.float32
     )

time: 473 us -> 447 us (0.945)
  blocking collectives: 48.2 us -> 0 us
  waiting for transfers between devices: 302 us -> 319 us
  starting transfers between devices: 23 us -> 28 us
    all_gather x1 -> x0, blocking collectives: 48.2 us -> none  [per_device(): positives = lax.all_gather(positive_clusters, 'label', axis=0, tiled=True)]
    all_to_all x1, waiting for transfers between devices: 39.4 us -> 52.9 us  [per_device(): lax.all_to_all(back.reshape(label_count, blocks_dev * capacity, width), '...]
    all_to_all x0 -> x1, waiting for transfers between devices: none -> 9.76 us  [per_device(): lax.all_to_all(jnp.stack([positive_clusters] * lax.axis_size('label')), '...]
    reduce_scatter x1, waiting for transfers between devices: 194 us -> 187 us  [per_device(): lax.psum_scatter(products.astype(jnp.bfloat16), 'label', scatter_dimensio...]
    all_to_all x0 -> x1, starting transfers between devices: none -> 6.34 us  [per_device(): lax.all_to_all(jnp.stack([positive_clusters] * lax.axis_size('label')), '...]
  transfers between devices with their start and end apart: 7 -> 8, of which waited for: 4 -> 5; matrix products, arithmetic and copies ran while one was open for 16% -> 17% of each run, Pallas kernels for 0% -> 0%
where the time goes in v1:
time: 447 us; the launch traced here: 446 us
  waiting for transfers between devices  319 us (71%)
  local copies, waits for them, and re-layouts  38.9 us (9%)
  matrix products  31.3 us (7%)
  starting transfers between devices  28 us (6%)
  between operations  15.9 us (4%)
  other arithmetic  13.4 us (3%)
    reduce_scatter x1, waiting for transfers between devices, per_device(): lax.psum_scatter(products.astype(jnp.bfloat16), 'label', scatter_dimensio...  187 us
    all_to_all x1, waiting for transfers between devices, per_device(): lax.all_to_all(send_rows, 'label', split_axis=0, concat_axis=0, tiled=True)  63.9 us
    all_to_all x1, waiting for transfers between devices, per_device(): lax.all_to_all(back.reshape(label_count, blocks_dev * capacity, width), '...  52.9 us
    unnamed x18, local copies, waits for them, and re-layouts  15.5 us
    all_to_all x1, starting transfers between devices, per_device(): lax.all_to_all(send_offsets, 'label', split_axis=0, concat_axis=0, tiled=...  11.3 us
    all_to_all x1, waiting for transfers between devices, per_device(): lax.all_to_all(jnp.stack([positive_clusters] * lax.axis_size('label')), '...  9.76 us
    dot_general x1, matrix products, per_device(): lax.dot_general(rows, cluster_weight, (((1,), (1,)), ((), ())), preferred...  9.33 us
    dot_general x1, matrix products, per_device(): jnp.dot(deltas, cluster_weight, preferred_element_type=jnp.float32)  8.97 us
  transfers between devices with their start and end apart: 8, of which 5 were waited for; matrix products, arithmetic and copies ran while one was open for 17% of the time, Pallas kernels for 0%

profile of v1, /device:TPU:8, one launch (start us, length us, event | category | flops | bytes accessed | tf_op | source)
XLA Modules:
  0.0 445.9 jit_solution(13350987079853864371)
XLA Ops:
  8.1 0.7 all-gather.2.cloned.1.call-update
  8.8 0.8 copy.45
  9.5 0.7 broadcast_multiply_fusion
  10.2 0.1 copy.44
  10.3 0.1 mul.37
  10.5 0.8 copy.46
  11.2 0.1 reshape.94
  11.4 0.1 eq.45
  11.5 0.5 fusion.8
  12.0 2.4 scatter_custom_fusion
  14.5 6.9 %gather_fusion = s32[1024]{0:T(1024)S(1)} fusion(s32[512]{0:T(512)S(1)} %reshape.94, s32[1024]{0:T(1024)S(1)} %maximum_clamp_fusion), kind=kCustom, calls=%fused_computation | custom fusion | bytes 12288 | tf_op jit(solution)/shard_map/gather | solution.py:57
  21.4 0.7 all_to_all.16
  22.1 11.3 %all-to-all-start.1 = ((s32[32,1,32]{2,1,0:T(1,128)}), s32[32,1,32]{2,1,0:T(1,128)S(1)}, u32[]{:S(2)}, u32[]{:S(2)}) async-start(s32[32,1,32]{2,1,0:T(1,128)} %bitcast.3), calls=%async_computation.2 | async-start | bytes 32768 | tf_op jit(solution)/shard_map/all_to_all | solution.py:62
  33.5 4.1 gather_fusion.1
  37.5 1.6 broadcast_select_fusion
  39.1 4.1 all-to-all-done.1
  43.2 5.7 %all-to-all-start.2 = ((bf16[32,32,1024]{2,1,0:T(8,128)(2,1)}), bf16[32,32,1024]{2,1,0:T(8,128)(2,1)S(1)}, u32[]{:S(2)}, u32[]{:S(2)}) async-start(bf16[32,32,1024]{2,1,0:T(8,128)(2,1)} %broadcast_select_fusion), calls=%async_computation.3 | async-start | bytes 4194304 | tf_op jit(solution)/shard_map/all_to_all | solution.py:61
  49.1 63.9 %all-to-all-done.2 = bf16[32,32,1024]{2,1,0:T(8,128)(2,1)S(1)} async-done(((bf16[32,32,1024]{2,1,0:T(8,128)(2,1)}), bf16[32,32,1024]{2,1,0:T(8,128)(2,1)S(1)}, u32[]{:S(2)}, u32[]{:S(2)}) %all-to-all-start.2) | async-done | bytes 2097184 | tf_op jit(solution)/shard_map/all_to_all | solution.py:61
  113.0 1.2 copy.49
  114.1 1.2 copy-done.2
  115.3 1.7 fusion.30
  117.0 3.2 fusion
  120.3 6.5 %copy.55 = bf16[2048,1024]{0,1:T(8,128)(2,1)} copy(bf16[2048,1024]{1,0:T(8,128)(2,1)} %bitcast.69) | data formatting | bytes 8388608
  126.8 0.7 copy-done.3
  127.4 0.6 stack.2
  128.1 6.3 %all-to-all-start = ((s32[32,128,4]{1,2,0:T(4,128)}), s32[32,128,4]{1,2,0:T(4,128)S(1)}, u32[]{:S(2)}, u32[]{:S(2)}) async-start(s32[32,128,4]{1,2,0:T(4,128)} %stack.2), calls=%async_computation | async-start | bytes 131072 | tf_op jit(solution)/shard_map/all_to_all | solution.py:20
  134.4 0.2 reduce-scatter.10.cloned.1.call-start
  134.7 9.8 %all-to-all-done = s32[32,128,4]{1,2,0:T(4,128)S(1)} async-done(((s32[32,128,4]{1,2,0:T(4,128)}), s32[32,128,4]{1,2,0:T(4,128)S(1)}, u32[]{:S(2)}, u32[]{:S(2)}) %all-to-all-start) | async-done | bytes 65568 | tf_op jit(solution)/shard_map/all_to_all | solution.py:20
  144.4 5.1 %compare_reduce_fusion = pred[4096,512]{1,0:T(8,128)(4,1)S(1)} fusion(s32[512]{0:T(512)S(1)} %iota_add_fusion, s32[4096,4]{0,1:T(4,128)S(1)} %bitcast.77), kind=kLoop, calls=%fused_computation.4 | loop fusion | flops 14680064 | bytes 2164736 | tf_op jit(solution)/shard_map/reduce_or | solution.py:26
  149.6 9.3 %subtract_convert_fusion = bf16[4096,512]{1,0:T(8,128)(2,1)S(1)} fusion(pred[4096,512]{1,0:T(8,128)(4,1)S(1)} %compare_reduce_fusion, bf16[4096,1024]{1,0:T(8,128)(2,1)} %all-gather.2.cloned.1.call-done, bf16[512,1024]{1,0:T(8,128)(2,1)S(1)} %copy-done), kind=kOutput, calls=%fused_computation.7 | convolution fusion | flops 4307550208 | bytes 15728640 | tf_op jit(solution)/shard_map/dot_general | solution.py:23
  159.0 1.9 copy-done.5
  160.9 4.5 %multiply_convert_fusion = bf16[512,1024]{1,0:T(8,128)(2,1)S(1)} fusion(bf16[4096,512]{1,0:T(8,128)(2,1)S(1)} %subtract_convert_fusion, bf16[4096,1024]{1,0:T(8,128)(2,1)S(1)} %copy-done.4), kind=kOutput, calls=%fused_computation.13 | convolution fusion | flops 4296015872 | bytes 13631488 | tf_op jit(solution)/shard_map/dot_general | solution.py:28
  165.4 1.3 copy.53
  166.8 0.3 reduce-scatter.8.cloned.1.call-start
  167.0 9.0 %convolution_convert_fusion = bf16[4096,1024]{1,0:T(8,128)(2,1)} fusion(bf16[4096,512]{1,0:T(8,128)(2,1)} %copy-done.5, bf16[512,1024]{1,0:T(8,128)(2,1)S(1)} %copy-done), kind=kOutput, calls=%fused_computation.8 | convolution fusion | flops 4299161600 | bytes 13631488 | tf_op jit(solution)/shard_map/dot_general | solution.py:33
  176.0 3.0 fusion.5
  179.0 2.5 copy.50
  181.5 4.0 all-to-all-start.3
  185.5 52.9 %all-to-all-done.3 = bf16[32,32,1024]{2,1,0:T(8,128)(2,1)S(1)} async-done(((bf16[32,32,1024]{2,1,0:T(8,128)(2,1)}), bf16[32,32,1024]{2,1,0:T(8,128)(2,1)S(1)}, u32[]{:S(2)}, u32[]{:S(2)}) %all-to-all-start.3) | async-done | bytes 2097184 | tf_op jit(solution)/shard_map/all_to_all | solution.py:75
  238.4 2.8 gather_fusion.2
  241.2 1.7 reshape.101
  242.9 2.2 reduce_sum.19
  245.1 1.3 copy.56
  246.5 1.1 convert.2
  247.5 1.0 copy.54
  248.6 0.7 convert_element_type.83
  249.3 187.2 %reduce-scatter.8.cloned.1.call-done = bf16[128,1024]{1,0:T(8,128)(2,1)} async-done(((bf16[4096,1024]{1,0:T(8,128)(2,1)}), bf16[128,1024]{1,0:T(8,128)(2,1)}) %reduce-scatter.8.cloned.1.call-update) | async-done | bytes 262160 | tf_op jit(solution)/shard_map/reduce_scatter | solution.py:34
  436.5 1.9 add_convert_fusion
  (27 shorter events, 0.4 us)
Async XLA Ops:
  8.0 141.6 %copy-start = (bf16[512,1024]{1,0:T(8,128)(2,1)S(1)}, bf16[512,1024]{1,0:T(8,128)(2,1)}, u32[]{:S(2)}) copy-start(bf16[512,1024]{1,0:T(8,128)(2,1)} %param.8) | copy-start | bytes 3145732
  8.0 25.5 %copy-start.1 = (bf16[128,1024]{1,0:T(8,128)(2,1)S(1)}, bf16[128,1024]{1,0:T(8,128)(2,1)}, u32[]{:S(2)}) copy-start(bf16[128,1024]{1,0:T(8,128)(2,1)} %param.6) | copy-start | bytes 786436
  8.0 141.6 %all-gather.2.cloned.1.call-start = ((), (), s32[]{:S(2)}) async-start(), calls=%async_computation.7 | async-start | bytes 8650752 | tf_op jit(solution)/shard_map/all_gather | solution.py:18
  22.1 21.1 %all-to-all-start.1 = ((s32[32,1,32]{2,1,0:T(1,128)}), s32[32,1,32]{2,1,0:T(1,128)S(1)}, u32[]{:S(2)}, u32[]{:S(2)}) async-start(s32[32,1,32]{2,1,0:T(1,128)} %bitcast.3), calls=%async_computation.2 | async-start | bytes 32768 | tf_op jit(solution)/shard_map/all_to_all | solution.py:62
  43.2 69.8 %all-to-all-start.2 = ((bf16[32,32,1024]{2,1,0:T(8,128)(2,1)}), bf16[32,32,1024]{2,1,0:T(8,128)(2,1)S(1)}, u32[]{:S(2)}, u32[]{:S(2)}) async-start(bf16[32,32,1024]{2,1,0:T(8,128)(2,1)} %broadcast_select_fusion), calls=%async_computation.3 | async-start | bytes 4194304 | tf_op jit(solution)/shard_map/all_to_all | solution.py:61
  48.9 196.2 %reduce-scatter.12.cloned.1.call-start = ((), (), s32[]{:S(2)}) async-start(), calls=%async_computation.10 | async-start | bytes 4718592
  113.0 2.3 copy-start.2
  126.7 0.7 copy-start.3
  128.1 16.4 %all-to-all-start = ((s32[32,128,4]{1,2,0:T(4,128)}), s32[32,128,4]{1,2,0:T(4,128)S(1)}, u32[]{:S(2)}, u32[]{:S(2)}) async-start(s32[32,128,4]{1,2,0:T(4,128)} %stack.2), calls=%async_computation | async-start | bytes 131072 | tf_op jit(solution)/shard_map/all_to_all | solution.py:20
  134.4 113.1 %reduce-scatter.10.cloned.1.call-start = ((), (), s32[]{:S(2)}) async-start(), calls=%async_computation.9 | async-start | bytes 1179648
  149.6 11.3 %copy-start.4 = (bf16[4096,1024]{1,0:T(8,128)(2,1)S(1)}, bf16[4096,1024]{1,0:T(8,128)(2,1)}, u32[]{:S(2)}) copy-start(bf16[4096,1024]{1,0:T(8,128)(2,1)} %all-gather.2.cloned.1.call-done) | copy-start | bytes 25165828
  159.0 1.9 copy-start.5
  166.8 269.7 %reduce-scatter.8.cloned.1.call-start = ((), (), s32[]{:S(2)}) async-start(), calls=%async_computation.8 | async-start | bytes 8650752 | tf_op jit(solution)/shard_map/reduce_scatter | solution.py:34
  181.5 56.9 %all-to-all-start.3 = ((bf16[32,32,1024]{2,1,0:T(8,128)(2,1)}), bf16[32,32,1024]{2,1,0:T(8,128)(2,1)S(1)}, u32[]{:S(2)}, u32[]{:S(2)}) async-start(bf16[32,32,1024]{2,1,0:T(8,128)(2,1)} %copy.50), calls=%async_computation.4 | async-start | bytes 4194304 | tf_op jit(solution)/shard_map/all_to_all | solution.py:75
Sparse Core Ops, SparseCore 0:
  11.4 126.5 all-gather.1
Sparse Core Ops, SparseCore 1:
  126.9 34.7 reduce-scatter.11
  166.8 30.6 reduce-scatter.9
  201.4 235.0 reduce-scatter.7
